TPU v7x, 128 devices: a whole 4x4x4 slice. The times are simulated.
128 devices in a mesh: worker: 4 (over x_lo, core), fsdp: 32 (over x_hi, y, z).
Axes of the slice: x: 4 (x_hi: 2, x_lo: 2; x = x_hi * 2 + x_lo), y: 4, z: 4, core: 2. Of those that a mesh axis runs over, the one named last changes fastest.
Arguments:
- out_grad: bfloat16 [65536, 4096], P(('worker', 'fsdp')), may hold values from -0.1875 to 0.1875
- hidden: bfloat16 [65536, 2048], P(('worker', 'fsdp')), may hold values from -6 to 6
- inner_param: float32 [4, 4096, 2048], P('worker', 'fsdp'), may hold values from -6 to 6
- adam_m: float32 [4, 4096, 2048], P('worker', 'fsdp'), may hold values from -6 to 6
- adam_v: float32 [4, 4096, 2048], P('worker', 'fsdp'), may hold values from 0.25 to 4
- old_inner: float32 [4, 4096, 2048], P('worker', 'fsdp'), may hold values from -6 to 6
- outer_param: float32 [4096, 2048], P('fsdp', 'worker'), may hold values from -6 to 6
- outer_mom: float32 [4096, 2048], P('fsdp', 'worker'), may hold values from -6 to 6
Outputs:
- param_next: float32 [4, 4096, 2048], P('worker', 'fsdp')
- first_next: float32 [4, 4096, 2048], P('worker', 'fsdp')
- second_next: float32 [4, 4096, 2048], P('worker', 'fsdp')
- outer_next: float32 [4096, 2048], P('fsdp', 'worker')
- moment_next: float32 [4096, 2048], P('fsdp', 'worker')
All inputs are finite; a program needn't handle non-finite values.
Results may differ from a plain program's by a relative error of at most 0.0003.
Values may be sent and summed in bfloat16 or wider, within the bound.
A program may use at most 192 MiB of HBM per device.

v0:
```python
import jax
import jax.numpy as jnp
from jax import lax
from jax.sharding import PartitionSpec as P

beta_one = 0.9
beta_two = 0.95
inner_step = 11
adam_eps = 1e-08
inner_rate = 0.3
decay_rate = 0.1
outer_rate = 0.7
outer_moment = 0.9


def adam_step(param, first_moment, second_moment, gradient):
    first_new = beta_one * first_moment + (1.0 - beta_one) * gradient
    second_new = beta_two * second_moment + (1.0 - beta_two) * gradient * gradient
    first_hat = first_new / (1.0 - beta_one**inner_step)
    second_hat = second_new / (1.0 - beta_two**inner_step)
    param_new = param - inner_rate * (
        first_hat / (jnp.sqrt(second_hat) + adam_eps) + decay_rate * param
    )
    return (param_new, first_new, second_new)


def nesterov(outer_param, outer_mom, outer_delta):
    moment_new = outer_moment * outer_mom + outer_delta
    outer_new = outer_param - outer_rate * (outer_delta + outer_moment * moment_new)
    return (outer_new, moment_new)


def per_device(out_grad, hidden, inner_param, adam_m, adam_v, old_inner, outer_param, outer_mom):
    gradient = lax.psum_scatter(
        lax.dot_general(
            out_grad, hidden, (((0,), (0,)), ((), ())), preferred_element_type=jnp.float32
        ),
        "fsdp",
        scatter_dimension=0,
        tiled=True,
    )
    param_next, first_next, second_next = adam_step(inner_param, adam_m, adam_v, gradient[None])
    own_old = old_inner[0]
    share_cols = outer_param.shape[1]
    summed = lax.psum(own_old, "worker")
    share_sum = lax.dynamic_slice_in_dim(
        summed, lax.axis_index("worker") * share_cols, share_cols, 1
    )
    outer_delta = outer_param - share_sum * (1.0 / lax.axis_size("worker"))
    outer_next, moment_next = nesterov(outer_param, outer_mom, outer_delta)
    return (param_next, first_next, second_next, outer_next, moment_next)


def solution(mesh):
    in_specs = (
        P(("worker", "fsdp"), None),
        P(("worker", "fsdp"), None),
        P("worker", "fsdp", None),
        P("worker", "fsdp", None),
        P("worker", "fsdp", None),
        P("worker", "fsdp", None),
        P("fsdp", "worker"),
        P("fsdp", "worker"),
    )
    out_specs = (
        P("worker", "fsdp", None),
        P("worker", "fsdp", None),
        P("worker", "fsdp", None),
        P("fsdp", "worker"),
        P("fsdp", "worker"),
    )
    return jax.shard_map(
        per_device, mesh=mesh, in_specs=in_specs, out_specs=out_specs, check_vma=False
    )
```

profile of v0, /device:TPU:0, one launch (start us, length us, event | category | flops | bytes accessed | tf_op | source)
XLA Modules:
  0.0 416.0 jit_solution(14743828288656182038)
XLA Ops:
  8.0 0.0 copy-start
  8.0 0.0 all-reduce.2.cloned.1.call-start
  8.1 0.7 all-reduce.2.cloned.1.call-update
  8.7 0.0 reduce-scatter.2.cloned.1.call-start
  8.8 0.8 copy-done
  9.6 17.7 %fusion.3 = f32[4096,2048]{1,0:T(8,128)} fusion(bf16[512,4096]{1,0:T(8,128)(2,1)} %param.8, bf16[512,2048]{1,0:T(8,128)(2,1)S(1)} %copy-done), kind=kOutput, calls=%fused_computation.8 | convolution fusion | flops 8589934592 | bytes 39845888 | tf_op jit(solution)/shard_map/dot_general | solution.py:35
  27.3 0.0 copy-start.2
  27.3 0.0 copy-start.1
  27.3 0.0 reduce-scatter.2.cloned.1.call-update
  27.4 46.7 %all-reduce.2.cloned.1.call-done = f32[128,2048]{1,0:T(8,128)} async-done(((f32[128,2048]{1,0:T(8,128)}), f32[128,2048]{1,0:T(8,128)}) %all-reduce.2.cloned.1.call-update) | async-done | bytes 1048592 | tf_op jit(solution)/shard_map/psum | solution.py:45
  74.1 0.0 copy-done.2
  74.1 1.9 multiply_subtract_fusion.1
  76.0 328.5 %reduce-scatter.2.cloned.1.call-done = f32[128,2048]{1,0:T(8,128)} async-done(((f32[4096,2048]{1,0:T(8,128)}), f32[128,2048]{1,0:T(8,128)}) %reduce-scatter.2.cloned.1.call-update) | async-done | bytes 1048592 | tf_op jit(solution)/shard_map/reduce_scatter | solution.py:34
  404.5 0.0 copy-done.1
  404.5 4.1 multiply_subtract_fusion
Async XLA Ops:
  8.0 1.6 copy-start
  8.0 66.1 %all-reduce.2.cloned.1.call-start = ((), (), s32[]{:S(2)}) async-start(), calls=%async_computation.2 | async-start | bytes 2097152 | tf_op jit(solution)/shard_map/psum | solution.py:45
  8.7 395.7 %reduce-scatter.2.cloned.1.call-start = ((), (), s32[]{:S(2)}) async-start(), calls=%async_computation.1 | async-start | bytes 34603008 | tf_op jit(solution)/shard_map/reduce_scatter | solution.py:34
  27.3 46.8 %copy-start.2 = (f32[128,512]{1,0:T(8,128)S(1)}, f32[128,512]{1,0:T(8,128)}, u32[]{:S(2)}) copy-start(f32[128,512]{1,0:T(8,128)} %param.14) | copy-start | bytes 786436
  27.3 377.1 %copy-start.1 = (f32[1,128,2048]{2,1,0:T(8,128)S(1)}, f32[1,128,2048]{2,1,0:T(8,128)}, u32[]{:S(2)}) copy-start(f32[1,128,2048]{2,1,0:T(8,128)} %param.10) | copy-start | bytes 3145732
Sparse Core Ops, SparseCore 0:
  11.4 62.6 all-reduce.1
Sparse Core Ops, SparseCore 1:
  27.5 377.0 reduce-scatter.1
where the time goes:
time: 417 us; the launch traced here: 416 us
  waiting for transfers between devices  376 us (90%)
  matrix products  17.7 us (4%)
  between operations  15.5 us (4%)
  other arithmetic  6.01 us (1%)
    reduce_scatter x1, waiting for transfers between devices, per_device(): lax.psum_scatter(lax.dot_general(out_grad, hidden, (((0,), (0,)), ((), ()...  328 us
    psum x1, waiting for transfers between devices, per_device(): summed = lax.psum(own_old, 'worker')  46.7 us
    dot_general x1, matrix products, per_device(): lax.dot_general(out_grad, hidden, (((0,), (0,)), ((), ())), preferred_ele...  17.7 us
  transfers between devices with their start and end apart: 2, of which 2 were waited for; matrix products, arithmetic and copies ran while one was open for 5% of the time, Pallas kernels for 0%

commit v1 on v0

v1 whole, which is shorter than its diff:
```python
import functools

import jax
import jax.numpy as jnp
from jax import lax
from jax.experimental import pallas as pl
from jax.experimental.pallas import tpu as pltpu
from jax.sharding import PartitionSpec as P

beta_one = 0.9
beta_two = 0.95
inner_step = 11
adam_eps = 1e-08
inner_rate = 0.3
decay_rate = 0.1
outer_rate = 0.7
outer_moment = 0.9

MESH = pl.DeviceIdType.MESH
ROWS = 128
COLS = 2048
TOK = 512
SHARE = 512
WIDE = 1024
SIDE = 128
MAIN = WIDE - SIDE
EXTRA = 128
SPLIT = MAIN - EXTRA
HALF = ROWS // 2
ITEMS = ((1, 2), (1, 1), (1, 3), (1, 0), (0, 2), (0, 1), (0, 3), (0, 0))
N_ITEM = len(ITEMS)
PIECES = 4
PIECE = ROWS // PIECES
PRE_ORDER = ((10, 6), (14, 9, 11), (2, 8, 5), (7, 13, 15), (1, 3, 4, 12, 0))
SCHEDULE = (
    "F0", "P0", "F1", "P1", "F2", "P2", "S0", "P3", "F3", "S1", "P4", "O", "T0",
    "F4", "S2", "T1", "F5", "S3", "T2", "F6", "S4", "T3", "F7", "R", "S5", "T4",
    "S6", "T5", "S7", "T6", "Q", "U", "T7",
)


def rel(stream, dx, da, db):
    return dx * 16 + (da * 4 + db if stream == 0 else db * 4 + da)


def block_order():
    order = []
    for step in SCHEDULE:
        kind, number = step[0], int(step[1:] or 0)
        if kind == "P":
            order += [16 + r for r in PRE_ORDER[number]]
        elif kind in "FST":
            dx, db = ITEMS[number]
            for s in (0, 1):
                order += [rel(s, dx, da, db) for da in {"F": (2,), "S": (1, 3), "T": (0,)}[kind]]
    return list(dict.fromkeys(order))


def adam_step(param, first_moment, second_moment, gradient):
    first_new = beta_one * first_moment + (1.0 - beta_one) * gradient
    second_new = beta_two * second_moment + (1.0 - beta_two) * gradient * gradient
    first_hat = first_new / (1.0 - beta_one**inner_step)
    second_hat = second_new / (1.0 - beta_two**inner_step)
    param_new = param - inner_rate * (
        first_hat / (jnp.sqrt(second_hat) + adam_eps) + decay_rate * param
    )
    return (param_new, first_new, second_new)


def nesterov(outer_param, outer_mom, outer_delta):
    moment_new = outer_moment * outer_mom + outer_delta
    outer_new = outer_param - outer_rate * (outer_delta + outer_moment * moment_new)
    return (outer_new, moment_new)


def encode(value):
    value = value * jnp.abs(value)
    return (value * jnp.abs(value)).astype(jnp.bfloat16)


def signed_root(value):
    return value * lax.rsqrt(jnp.maximum(jnp.abs(value), 1e-30))


def decode(code):
    return signed_root(signed_root(code.astype(jnp.float32)))


def kernel(
    a_hbm,
    b_hbm,
    old_hbm,
    p_hbm,
    m_hbm,
    v_hbm,
    op_hbm,
    om_hbm,
    pn_ref,
    mn_ref,
    vn_ref,
    on_ref,
    omn_ref,
    a_ref,
    b_ref,
    bx_ref,
    at_ref,
    own_ref,
    peers_ref,
    pair_ref,
    last_ref,
    state_ref,
    ostate_ref,
    pre_out,
    pre_in,
    pre_sum,
    extra_out,
    extra_in,
    s1_out0,
    s1_in0,
    s1_out1,
    s1_in1,
    m2_out0,
    m2_in0,
    m2_out1,
    m2_in1,
    x_out,
    x_in,
    t1_out,
    t1_in,
    t2_out,
    t2_in,
    load_sem,
    a_sem,
    state_sem,
    ostate_sem,
    p_ss,
    p_rs,
    s1_ss,
    s1_rs,
    m2_ss,
    m2_rs,
    x_ss,
    x_rs,
    t1_ss,
    t1_rs,
    t2_ss,
    t2_rs,
    o_ss,
    o_rs,
    l_ss,
    l_rs,
    e_ss,
    e_rs,
):
    s1_out, s1_in = (s1_out0, s1_out1), (s1_in0, s1_in1)
    m2_out, m2_in = (m2_out0, m2_out1), (m2_in0, m2_in1)
    w = lax.axis_index("worker")
    f = lax.axis_index("fsdp")
    px, py, pz = f // 16, (f // 4) % 4, f % 4

    def place(dx, dy, dz):
        return ((px + dx) % 2) * 16 + ((py + dy) % 4) * 4 + (pz + dz) % 4

    def near(stream, axis, way):
        along_y = (stream == 0) == (axis == 0)
        return (w, place(0, way, 0) if along_y else place(0, 0, way))

    across = (w, place(1, 0, 0))
    sibling, beside = (w // 2 * 2 + 1 - w % 2, f), ((w + 2) % 4, f)

    def strip(r):
        start = place(r // 16, (r // 4) % 4, r % 4) * ROWS
        return pl.ds(pl.multiple_of(start, ROWS), ROWS)

    loads = {
        r: pltpu.make_async_copy(a_hbm.at[:, strip(r)], a_ref.at[r], a_sem.at[r])
        for r in block_order()
    }
    b_loads = [
        pltpu.make_async_copy(
            b_hbm.at[:, pl.ds(s * WIDE, WIDE)], b_ref.at[s], load_sem.at[s]
        )
        for s in (0, 1)
    ]
    waiting = list(loads.values())
    for load in waiting[:1] + b_loads:
        load.start()

    barrier = pltpu.get_barrier_semaphore()
    friends = [near(0, 0, 1), near(0, 0, 3), near(1, 0, 1), near(1, 0, 3), across, sibling, beside]
    for friend in friends:
        pl.semaphore_signal(barrier, inc=1, device_id=friend, device_id_type=MESH)
    for load in waiting[1:]:
        load.start()
    pl.semaphore_wait(barrier, len(friends))

    started = []

    def send(src, dst, ssem, rsem, device):
        copy = pltpu.make_async_remote_copy(
            src_ref=src,
            dst_ref=dst,
            send_sem=ssem,
            recv_sem=rsem,
            device_id=device,
            device_id_type=MESH,
        )
        copy.start()
        started.append(copy)
        return copy

    def drain(keep):
        done = started[:keep]
        for copy in done:
            copy.wait_send()
        del started[: len(done)]

    turned = set()

    def turn(r):
        if r not in turned:
            turned.add(r)
            loads[r].wait()
            at_ref[r] = a_ref[r].T

    def product(r, columns):
        turn(r)
        return jnp.dot(at_ref[r], columns, preferred_element_type=jnp.float32)

    loaded = set()

    def right(s, lo, hi):
        if s not in loaded:
            loaded.add(s)
            b_loads[s].wait()
        return b_ref[s, :, lo:hi]

    def parts(s, dx, da, db, split=False):
        r = rel(s, dx, da, db)
        for lo, hi in ((0, SPLIT), (SPLIT, MAIN)) if split else ((0, MAIN),):
            yield pl.ds(lo, hi - lo), product(r, right(s, lo, hi))
        if dx == 0:
            pre_ready(r)
            yield pl.ds(MAIN, SIDE), pre_sum[r, :, s * SIDE : (s + 1) * SIDE]

    pre, summed_pre = {}, set()

    def pre_send(batch):
        if batch == 0:
            for s in (0, 1):
                bx_ref[:, s * SIDE : (s + 1) * SIDE] = right(s, MAIN, WIDE)
        for r in PRE_ORDER[batch]:
            pre_out[r] = encode(product(16 + r, bx_ref[...]))
            pre[r] = send(pre_out.at[r], pre_in.at[r], p_ss.at[r], p_rs.at[r], across)

    def pre_ready(r):
        if r not in summed_pre:
            summed_pre.add(r)
            pre[r].wait_recv()
            pre_sum[r] = product(r, bx_ref[...]) + decode(pre_in[r])

    s1, m2, xs, t1, t2, last, extra = {}, {}, {}, {}, {}, {}, {}

    def top(d):
        return slice(d * HALF, (d + 1) * HALF)

    def piece(h):
        return pl.ds(h * PIECE, PIECE)

    def first(k):
        dx, db = ITEMS[k]
        width = SPLIT if (dx, db) == (1, 0) else MAIN + (1 - dx) * SIDE
        for s in (0, 1):
            for cols, value in parts(s, dx, 2, db, db == 0):
                if db == 0 and cols.start == SPLIT:
                    if dx == 1:
                        extra_out[s] = encode(value)
                        extra[s] = send(
                            extra_out.at[s], extra_in.at[s], e_ss.at[s], e_rs.at[s], across
                        )
                        continue
                    extra[s].wait_recv()
                    value += decode(extra_in[s])
                for d in (0, 1):
                    s1_out[dx][s, db, d, :, cols] = encode(value[top(d)])
            for d in (0, 1):
                s1[s, k, d] = send(
                    s1_out[dx].at[s, db, d, :, pl.ds(0, width)],
                    s1_in[dx].at[s, db, d, :, pl.ds(0, width)],
                    s1_ss.at[s, k, d],
                    s1_rs.at[s, k, d],
                    near(s, 0, 3 if d else 1),
                )

    def second(k):
        dx, db = ITEMS[k]
        for s in (0, 1):
            for d in (0, 1):
                s1[s, k, d].wait_recv()
                split = (dx, db) == (1, 0)
                for cols, value in parts(s, dx, 3 if d else 1, db, split):
                    if split and cols.start == SPLIT:
                        m2_out[dx][s, db, d, :, cols] = encode(value)
                        continue
                    came = decode(s1_in[dx][s, db, d, :, cols])
                    m2_out[dx][s, db, d, top(d), cols] = encode(value[top(d)] + came)
                    m2_out[dx][s, db, d, top(1 - d), cols] = encode(value[top(1 - d)])
                if k == N_ITEM - 1:
                    for h in range(PIECES):
                        last[s, d, h] = send(
                            m2_out[dx].at[s, db, d, piece(h)],
                            m2_in[dx].at[s, db, d, piece(h)],
                            l_ss.at[s, d, h],
                            l_rs.at[s, d, h],
                            near(s, 0, 3 if d else 1),
                        )
                    continue
                m2[s, k, d] = send(
                    m2_out[dx].at[s, db, d],
                    m2_in[dx].at[s, db, d],
                    m2_ss.at[s, k, d],
                    m2_rs.at[s, k, d],
                    near(s, 0, 3 if d else 1),
                )

    def third(k):
        dx, db = ITEMS[k]
        for s in (0, 1):
            for d in (0, 1):
                m2[s, k, d].wait_recv()
            if dx == 0:
                xs[s, db].wait_recv()
            if dx == 0 and db in (1, 3):
                t1[s, db // 2].wait_recv()
            for cols, total in parts(s, dx, 0, db):
                total += decode(m2_in[dx][s, db, 0, :, cols])
                total += decode(m2_in[dx][s, db, 1, :, cols])
                if dx == 1:
                    x_out[s, db, :, cols] = encode(total)
                    continue
                if cols.start < MAIN:
                    total += decode(x_in[s, db, :, cols])
                if db == 2:
                    for d in (0, 1):
                        t1_out[s, d, :, cols] = encode(total[top(d)])
                else:
                    d = db // 2
                    came = decode(t1_in[s, d, :, cols])
                    t2_out[s, d, top(d), cols] = encode(total[top(d)] + came)
                    t2_out[s, d, top(1 - d), cols] = encode(total[top(1 - d)])
            if dx == 1:
                xs[s, db] = send(
                    x_out.at[s, db], x_in.at[s, db], x_ss.at[s, db], x_rs.at[s, db], across
                )
            elif db == 2:
                for d in (0, 1):
                    t1[s, d] = send(
                        t1_out.at[s, d],
                        t1_in.at[s, d],
                        t1_ss.at[s, d],
                        t1_rs.at[s, d],
                        near(s, 1, 3 if d else 1),
                    )
            else:
                d = db // 2
                for h in range(PIECES):
                    t2[s, d, h] = send(
                        t2_out.at[s, d, piece(h)],
                        t2_in.at[s, d, piece(h)],
                        t2_ss.at[s, d, h],
                        t2_rs.at[s, d, h],
                        near(s, 1, 3 if d else 1),
                    )

    def prepare():
        drain(-8 * PIECES)
        for s in (0, 1):
            xs[s, 0].wait_recv()
            for cols, value in parts(s, 0, 0, 0):
                if cols.start < MAIN:
                    value += decode(x_in[s, 0, :, cols])
                last_ref[s, :, cols] = value

    def finish():
        for h in range(PIECES):
            for s in (0, 1):
                for d in (0, 1):
                    t2[s, d, h].wait_recv()
                    last[s, d, h].wait_recv()
                total = last_ref[s, piece(h)]
                for d in (0, 1):
                    total += decode(t2_in[s, d, piece(h)])
                    total += decode(m2_in[0][s, 0, d, piece(h)])
                where = pl.ds(s * WIDE, WIDE)
                new = adam_step(*(state_ref[i, piece(h), where] for i in range(3)), total)
                for out, part in zip((pn_ref, mn_ref, vn_ref), new):
                    out[piece(h), where] = part

    core, chip = w % 2, w // 2
    outer = {}

    def share(worker):
        return old_hbm.at[:, pl.ds(pl.multiple_of(worker * SHARE, SHARE), SHARE)]

    own_loads = [
        pltpu.make_async_copy(share(w), own_ref.at[0], load_sem.at[2]),
        pltpu.make_async_copy(share((w + 2) % 4), own_ref.at[1], load_sem.at[3]),
    ]

    outer_loads = [
        pltpu.make_async_copy(src, ostate_ref.at[i], ostate_sem.at[i])
        for i, src in enumerate((op_hbm, om_hbm))
    ]
    state_loads = [
        pltpu.make_async_copy(src, state_ref.at[i], state_sem.at[i])
        for i, src in enumerate((p_hbm, m_hbm, v_hbm))
    ]

    def outer_send():
        for load in outer_loads + state_loads:
            load.start()
        for load in own_loads:
            load.start()
        for i in (0, 1):
            outer[i] = send(
                share((chip + i) % 2 * 2 + 1 - core), peers_ref.at[i], o_ss.at[i], o_rs.at[i], sibling
            )

    def outer_pass():
        for load in own_loads:
            load.wait()
        outer[1].wait_recv()
        pair_ref[...] = own_ref[1] + peers_ref[1]
        outer[2] = send(pair_ref, peers_ref.at[2], o_ss.at[2], o_rs.at[2], beside)

    def outer_sum():
        outer[0].wait_recv()
        outer[2].wait_recv()
        share_sum = (own_ref[0] + peers_ref[0]) + peers_ref[2]
        for load in outer_loads:
            load.wait()
        outer_delta = ostate_ref[0] - share_sum * (1.0 / 4)
        on_ref[...], omn_ref[...] = nesterov(ostate_ref[0], ostate_ref[1], outer_delta)
        for load in state_loads:
            load.wait()

    steps = {"F": first, "S": second, "T": third, "P": pre_send}
    for step in SCHEDULE:
        if step == "O":
            outer_send()
        elif step == "U":
            prepare()
        elif step == "T7":
            finish()
        elif step == "R":
            outer_pass()
        elif step == "Q":
            outer_sum()
        else:
            steps[step[0]](int(step[1:]))
    drain(None)


def step_all(out_grad, hidden, old_inner, *state):
    bf16, f32 = jnp.bfloat16, jnp.float32
    dma = pltpu.SemaphoreType.DMA
    anywhere = pl.BlockSpec(memory_space=pl.ANY)
    full = pltpu.VMEM((ROWS, COLS), f32)
    part = pltpu.VMEM((ROWS, SHARE), f32)
    return pl.pallas_call(
        kernel,
        out_shape=(full, full, full, part, part),
        in_specs=[anywhere] * 8,
        out_specs=(pl.BlockSpec(memory_space=pltpu.VMEM),) * 5,
        scratch_shapes=[
            pltpu.VMEM((32, TOK, ROWS), bf16),
            pltpu.VMEM((2, TOK, WIDE), bf16),
            pltpu.VMEM((TOK, 2 * SIDE), bf16),
            pltpu.VMEM((32, ROWS, TOK), bf16),
            pltpu.VMEM((2, ROWS, SHARE), f32),
            pltpu.VMEM((3, ROWS, SHARE), f32),
            pltpu.VMEM((ROWS, SHARE), f32),
            pltpu.VMEM((2, ROWS, WIDE), f32),
            pltpu.VMEM((3, ROWS, COLS), f32),
            pltpu.VMEM((2, ROWS, SHARE), f32),
            pltpu.VMEM((16, ROWS, 2 * SIDE), bf16),
            pltpu.VMEM((16, ROWS, 2 * SIDE), bf16),
            pltpu.VMEM((16, ROWS, 2 * SIDE), f32),
            pltpu.VMEM((2, ROWS, EXTRA), bf16),
            pltpu.VMEM((2, ROWS, EXTRA), bf16),
            pltpu.VMEM((2, 4, 2, HALF, WIDE), bf16),
            pltpu.VMEM((2, 4, 2, HALF, WIDE), bf16),
            pltpu.VMEM((2, 4, 2, HALF, MAIN), bf16),
            pltpu.VMEM((2, 4, 2, HALF, MAIN), bf16),
            pltpu.VMEM((2, 4, 2, ROWS, WIDE), bf16),
            pltpu.VMEM((2, 4, 2, ROWS, WIDE), bf16),
            pltpu.VMEM((2, 4, 2, ROWS, MAIN), bf16),
            pltpu.VMEM((2, 4, 2, ROWS, MAIN), bf16),
            pltpu.VMEM((2, 4, ROWS, MAIN), bf16),
            pltpu.VMEM((2, 4, ROWS, MAIN), bf16),
            pltpu.VMEM((2, 2, HALF, WIDE), bf16),
            pltpu.VMEM((2, 2, HALF, WIDE), bf16),
            pltpu.VMEM((2, 2, ROWS, WIDE), bf16),
            pltpu.VMEM((2, 2, ROWS, WIDE), bf16),
            dma((4,)),
            dma((32,)),
            dma((3,)),
            dma((2,)),
            dma((16,)),
            dma((16,)),
            dma((2, N_ITEM, 2)),
            dma((2, N_ITEM, 2)),
            dma((2, N_ITEM, 2)),
            dma((2, N_ITEM, 2)),
            dma((2, 4)),
            dma((2, 4)),
            dma((2, 2)),
            dma((2, 2)),
            dma((2, 2, PIECES)),
            dma((2, 2, PIECES)),
            dma((3,)),
            dma((3,)),
            dma((2, 2, PIECES)),
            dma((2, 2, PIECES)),
            dma((2,)),
            dma((2,)),
        ],
        compiler_params=pltpu.CompilerParams(
            collective_id=0, has_side_effects=True, vmem_limit_bytes=53 << 20
        ),
        cost_estimate=pl.CostEstimate(
            flops=2 * TOK * 32 * ROWS * COLS, bytes_accessed=10 << 20, transcendentals=0
        ),
        name="step_all",
    )(out_grad, hidden, old_inner, *state)


def write_kernel(*refs):
    ins, outs, sem = refs[:5], refs[5:10], refs[10]
    copies = [
        pltpu.make_async_copy(src, dst, sem.at[i]) for i, (src, dst) in enumerate(zip(ins, outs))
    ]
    for copy in copies:
        copy.start()
    for copy in copies:
        copy.wait()


def write_all(results):
    anywhere = pl.BlockSpec(memory_space=pl.ANY)
    return pl.pallas_call(
        write_kernel,
        out_shape=tuple(pltpu.HBM(r.shape, r.dtype) for r in results),
        in_specs=[anywhere] * 5,
        out_specs=(anywhere,) * 5,
        scratch_shapes=[pltpu.SemaphoreType.DMA((5,))],
        compiler_params=pltpu.CompilerParams(vmem_limit_bytes=1 << 20),
        name="write_all",
    )(*(pltpu.with_memory_space_constraint(r, pltpu.VMEM) for r in results))


def per_device(out_grad, hidden, inner_param, adam_m, adam_v, old_inner, outer_param, outer_mom):
    results = step_all(
        out_grad, hidden, old_inner[0], inner_param[0], adam_m[0], adam_v[0], outer_param, outer_mom
    )
    param_next, first_next, second_next, outer_next, moment_next = write_all(results)
    return (param_next[None], first_next[None], second_next[None], outer_next, moment_next)


def solution(mesh):
    in_specs = (
        P(("worker", "fsdp"), None),
        P(("worker", "fsdp"), None),
        P("worker", "fsdp", None),
        P("worker", "fsdp", None),
        P("worker", "fsdp", None),
        P("worker", "fsdp", None),
        P("fsdp", "worker"),
        P("fsdp", "worker"),
    )
    out_specs = (
        P("worker", "fsdp", None),
        P("worker", "fsdp", None),
        P("worker", "fsdp", None),
        P("fsdp", "worker"),
        P("fsdp", "worker"),
    )
    return jax.shard_map(
        per_device, mesh=mesh, in_specs=in_specs, out_specs=out_specs, check_vma=False
    )
```

time: 417 us -> 85.6 us (0.21)
  waiting for transfers between devices: 376 us -> 0 us
  Pallas kernels: 0 us -> 84.7 us
  matrix products: 17.7 us -> 0 us
  between operations: 15.5 us -> 0.82 us
  other arithmetic: 6.01 us -> 0 us
    reduce_scatter x1 -> x0, waiting for transfers between devices: 328 us -> none  [per_device(): lax.psum_scatter(lax.dot_general(out_grad, hidden, (((0,), (0,)), ((), ()...]
    pallas_call x0 -> x2, Pallas kernels: none -> 84.7 us  [the longest x1 82.8 us: step_all(): pl.pallas_call(kernel, out_shape=(full, full, full, part, part), in_specs...]
    psum x1 -> x0, waiting for transfers between devices: 46.7 us -> none  [per_device(): summed = lax.psum(own_old, 'worker')]
    dot_general x1 -> x0, matrix products: 17.7 us -> none  [per_device(): lax.dot_general(out_grad, hidden, (((0,), (0,)), ((), ())), preferred_ele...]
    sub x2 -> x0, other arithmetic: 6.01 us -> none  [the longest x1 4.1 us: adam_step(): param - inner_rate * (first_hat / (jnp.sqrt(second_hat) + adam_eps) + dec...]
  transfers between devices with their start and end apart: 2 -> 0, of which waited for: 2 -> 0; matrix products, arithmetic and copies ran while one was open for 5% -> 0% of each run, Pallas kernels for 0% -> 0%
where the time goes in v1:
time: 85.6 us; the launch traced here: 85.5 us
  Pallas kernels  84.7 us (99%)
    pallas_call x1, Pallas kernels, step_all(): pl.pallas_call(kernel, out_shape=(full, full, full, part, part), in_specs...  82.8 us
    pallas_call x1, Pallas kernels, write_all(): pl.pallas_call(write_kernel, out_shape=tuple((pltpu.HBM(r.shape, r.dtype)...  1.87 us

profile of v1, /device:TPU:0, one launch (start us, length us, event | category | flops | bytes accessed | tf_op | source)
XLA Modules:
  0.0 85.5 jit_solution(17724724593921444469)
XLA Ops:
  0.6 82.8 %step_all.1 = (f32[128,2048]{1,0:T(8,128)S(1)}, f32[128,2048]{1,0:T(8,128)S(1)}, f32[128,2048]{1,0:T(8,128)S(1)}, f32[128,512]{1,0:T(8,128)S(1)}, f32[128,512]{1,0:T(8,128)S(1)}) custom-call(bf16[512,4096]{1,0:T(8,128)(2,1)} %a_hbm.1, bf16[512,2048]{1,0:T(8,128)(2,1)} %b_hbm.1, f32[128,2048]{1,0:T(8,128)} %bitcast.7, f32[128,2048]{1,0:T(8,128)} %bitcast.8, ...), custom_call_target="tpu_custom_call" | custom-call | flops 8589934592 | bytes 10485760 | tf_op jit(solution)/shard_map/step_all/pallas_call | solution.py:470
  83.4 1.9 %write_all.1 = (f32[128,2048]{1,0:T(8,128)}, f32[128,2048]{1,0:T(8,128)}, f32[128,2048]{1,0:T(8,128)}, f32[128,512]{1,0:T(8,128)}, f32[128,512]{1,0:T(8,128)}) custom-call(f32[128,2048]{1,0:T(8,128)S(1)} %get-tuple-element.15.refs_0_, f32[128,2048]{1,0:T(8,128)S(1)} %get-tuple-element.16.refs_1_, f32[128,2048]{1,0:T(8,128)S(1)} %get-tuple-element.17.refs_2_, ...), custom_call_target="tpu_custom_call" | custom-call | tf_op jit(solution)/shard_map/write_all/pallas_call | solution.py:551

commit v2 on v1

--- a/solution.py
+++ b/solution.py
@@ -29,7 +29,7 @@
 HALF = ROWS // 2
 ITEMS = ((1, 2), (1, 1), (1, 3), (1, 0), (0, 2), (0, 1), (0, 3), (0, 0))
 N_ITEM = len(ITEMS)
-PIECES = 4
+PIECES = 2
 PIECE = ROWS // PIECES
 PRE_ORDER = ((10, 6), (14, 9, 11), (2, 8, 5), (7, 13, 15), (1, 3, 4, 12, 0))
 SCHEDULE = (

time: 85.6 us -> 85.7 us (level)
  no operation moved by 1% of the time
where the time goes in v2:
time: 85.7 us; the launch traced here: 85.6 us
  Pallas kernels  84.8 us (99%)
    pallas_call x1, Pallas kernels, step_all(): pl.pallas_call(kernel, out_shape=(full, full, full, part, part), in_specs...  82.9 us
    pallas_call x1, Pallas kernels, write_all(): pl.pallas_call(write_kernel, out_shape=tuple((pltpu.HBM(r.shape, r.dtype)...  1.87 us

profile of v2, /device:TPU:0, one launch (start us, length us, event | category | flops | bytes accessed | tf_op | source)
XLA Modules:
  0.0 85.6 jit_solution(8044838777359964877)
XLA Ops:
  0.6 82.9 %step_all.1 = (f32[128,2048]{1,0:T(8,128)S(1)}, f32[128,2048]{1,0:T(8,128)S(1)}, f32[128,2048]{1,0:T(8,128)S(1)}, f32[128,512]{1,0:T(8,128)S(1)}, f32[128,512]{1,0:T(8,128)S(1)}) custom-call(bf16[512,4096]{1,0:T(8,128)(2,1)} %a_hbm.1, bf16[512,2048]{1,0:T(8,128)(2,1)} %b_hbm.1, f32[128,2048]{1,0:T(8,128)} %bitcast.7, f32[128,2048]{1,0:T(8,128)} %bitcast.8, ...), custom_call_target="tpu_custom_call" | custom-call | flops 8589934592 | bytes 10485760 | tf_op jit(solution)/shard_map/step_all/pallas_call | solution.py:470
  83.6 1.9 %write_all.1 = (f32[128,2048]{1,0:T(8,128)}, f32[128,2048]{1,0:T(8,128)}, f32[128,2048]{1,0:T(8,128)}, f32[128,512]{1,0:T(8,128)}, f32[128,512]{1,0:T(8,128)}) custom-call(f32[128,2048]{1,0:T(8,128)S(1)} %get-tuple-element.15.refs_0_, f32[128,2048]{1,0:T(8,128)S(1)} %get-tuple-element.16.refs_1_, f32[128,2048]{1,0:T(8,128)S(1)} %get-tuple-element.17.refs_2_, ...), custom_call_target="tpu_custom_call" | custom-call | tf_op jit(solution)/shard_map/write_all/pallas_call | solution.py:551
